TPU v7x, 128 devices: a whole 4x4x4 slice. The times are simulated.
128 devices in a mesh: row: 8 (over y_hi, x), col: 16 (over y_lo, z, core).
Axes of the slice: x: 4, y: 4 (y_hi: 2, y_lo: 2; y = y_hi * 2 + y_lo), z: 4, core: 2. Of those that a mesh axis runs over, the one named last changes fastest.
Arguments:
- layer_input: bfloat16 [32768, 3072], P('col', 'row'), may hold values from -6 to 6
- conv_grad: bfloat16 [32768, 13312], P('col', 'row'), may hold values from -0.03125 to 0.03125
- conv_kernel: float32 [4, 13312], P(None, 'row'), may hold values from -3 to 3
- segment_ids: int32 [32768], P('col'), may hold values from 0 to 257, never falling along the last dimension, each value on 1 to 4096 neighbouring positions
- left_basis: float32 [3072, 192], P('col'), may hold values from -0.4375 to 0.4375
- right_basis: float32 [13312, 416], P('row'), may hold values from -0.3125 to 0.3125
- left_stat: float32 [3072, 192], P('col', 'row'), may hold values from -2 to 2
- right_stat: float32 [13312, 416], P('row', 'col'), may hold values from -2 to 2
- first_moment: float32 [3072, 13312], P('col', 'row'), may hold values from -0.6 to 0.6
- second_moment: float32 [3072, 13312], P('col', 'row'), may hold values from 0.005 to 0.05
Outputs:
- new_left_stat: float32 [3072, 192], P('col', 'row')
- new_right_stat: float32 [13312, 416], P('row', 'col')
- new_first: float32 [3072, 13312], P('col', 'row')
- new_second: float32 [3072, 13312], P('col', 'row')
- direction: float32 [3072, 13312], P('col', 'row')
Inputs may be any that keep to these rules, and one draw needn't show every extreme that they name: `segment_ids`: document numbers never fall along the tokens; each document holds 1 to 4096 tokens.
All inputs are finite; a program needn't handle non-finite values.
Results may differ from a plain program's by a relative error of at most 0.0023.
Values may be sent and summed in bfloat16 or wider, within the bound.
A program may use at most 320 MiB of HBM per device.

v0:
```python
import jax
import jax.numpy as jnp
from jax import lax
from jax.sharding import PartitionSpec as P

MODEL_WIDTH = 3072
OUTPUT_CHANNELS = 13312
ZW = 6144
XW = 6656


def passed_along(block, axis, distance):
    devices = range(lax.axis_size(axis))
    route = [(i - distance, i) for i in devices if i - distance in devices]
    return lax.ppermute(block, axis, route)


def contract_rows(left, right):
    return lax.dot_general(
        left, right, (((0,), (0,)), ((), ())), preferred_element_type=jnp.float32
    )


def conv_backward(conv_grad, conv_kernel, segment_ids):
    taps = conv_kernel.shape[0]
    count = conv_grad.shape[0]
    output_channel_columns = conv_grad.shape[1]
    after_grad, after_ids = passed_along(
        (conv_grad[: taps - 1], segment_ids[: taps - 1]), "col", -1
    )
    longer = jnp.concatenate([conv_grad, after_grad], 0)
    long_ids = jnp.concatenate([segment_ids, after_ids.astype(jnp.int32)], 0)
    plain = conv_grad.astype(jnp.float32)
    total = conv_kernel[0][None, :] * plain
    for offset in range(1, taps):
        same = long_ids[offset : offset + count] == segment_ids
        term = conv_kernel[offset][None, :] * longer[offset : offset + count].astype(jnp.float32)
        total = total + jnp.where(same[:, None], term, jnp.float32(0.0))
    channel = lax.axis_index("row") * output_channel_columns + jnp.arange(
        output_channel_columns, dtype=jnp.int32
    )
    convolved = (channel >= ZW) & (channel < ZW + XW)
    total = jnp.where(convolved[None, :], total, plain)
    return total.astype(jnp.bfloat16)


def shards(
    layer_input,
    conv_grad,
    conv_kernel,
    segment_ids,
    left_basis,
    right_basis,
    left_stat,
    right_stat,
    first_moment,
    second_moment,
):
    highest_precision = lax.Precision.HIGHEST
    proj_grad = conv_backward(conv_grad, conv_kernel, segment_ids)
    dcols = left_basis.shape[0]
    lblock = left_basis.shape[1]
    output_channel_columns = right_basis.shape[0]
    right_block_index = right_basis.shape[1]
    partial_grad = contract_rows(lax.all_gather(layer_input, "row", axis=1, tiled=True), proj_grad)
    grad = lax.psum_scatter(partial_grad, "col", scatter_dimension=0, tiled=True)
    nblocks = dcols // lblock
    nstrips = output_channel_columns // right_block_index
    blocks = grad.reshape(nblocks, lblock, output_channel_columns)
    left_term = (
        jnp.einsum("bie,bje->bij", blocks, blocks, precision=highest_precision).reshape(
            dcols, lblock
        )
        / OUTPUT_CHANNELS
    )
    column_bands = grad.reshape(dcols, nstrips, right_block_index)
    right_factor_term = (
        jnp.einsum("rtz,rtk->tzk", column_bands, column_bands, precision=highest_precision).reshape(
            output_channel_columns, right_block_index
        )
        / MODEL_WIDTH
    )
    left_sum = lax.psum(left_term.astype(jnp.bfloat16), "row").astype(jnp.float32)
    right_sum = lax.psum(right_factor_term.astype(jnp.bfloat16), "col").astype(jnp.float32)
    lwidth = left_stat.shape[1]
    rwidth = right_stat.shape[1]
    left_part = lax.dynamic_slice_in_dim(left_sum, lax.axis_index("row") * lwidth, lwidth, 1)
    right_part = lax.dynamic_slice_in_dim(right_sum, lax.axis_index("col") * rwidth, rwidth, 1)
    new_left_stat = 0.9 * left_stat + 0.1 * left_part
    new_right_stat = 0.9 * right_stat + 0.1 * right_part
    left_q = left_basis.reshape(nblocks, lblock, lblock)
    right_q = right_basis.reshape(nstrips, right_block_index, right_block_index)
    half = jnp.einsum("bki,bke->bie", left_q, blocks, precision=highest_precision).reshape(
        dcols, nstrips, right_block_index
    )
    rotated = jnp.einsum("dck,ckj->dcj", half, right_q, precision=highest_precision).reshape(
        dcols, output_channel_columns
    )
    new_first = 0.9 * first_moment + 0.1 * rotated
    new_second = 0.95 * second_moment + 0.05 * rotated * rotated
    scaled = new_first / (jnp.sqrt(new_second) + 1e-08)
    back = jnp.einsum(
        "bik,bke->bie",
        left_q,
        scaled.reshape(nblocks, lblock, output_channel_columns),
        precision=highest_precision,
    ).reshape(dcols, nstrips, right_block_index)
    direction = jnp.einsum("dck,cjk->dcj", back, right_q, precision=highest_precision).reshape(
        dcols, output_channel_columns
    )
    return (new_left_stat, new_right_stat, new_first, new_second, direction)


def solution(mesh):
    placed = (
        P("col", "row"),
        P("col", "row"),
        P(None, "row"),
        P("col"),
        P("col", None),
        P("row", None),
        P("col", "row"),
        P("row", "col"),
        P("col", "row"),
        P("col", "row"),
    )
    return jax.shard_map(
        shards,
        mesh=mesh,
        in_specs=placed,
        out_specs=(
            P("col", "row"),
            P("row", "col"),
            P("col", "row"),
            P("col", "row"),
            P("col", "row"),
        ),
        check_vma=False,
    )
```

profile of v0, /device:TPU:1, one launch (start us, length us, event | category | flops | bytes accessed | tf_op | source)
XLA Modules:
  0.0 555.0 jit_solution(9330108872627229990)
XLA Ops:
  7.2 0.0 copy-start
  7.2 0.0 all-gather.2.cloned.1.call-start
  7.2 0.7 all-gather.2.cloned.1.call-update
  7.9 0.0 reduce-scatter.4.cloned.1.call-start
  8.0 0.7 slice.37
  8.7 3.3 collective-permute-start
  12.0 0.8 slice.40
  12.7 1.9 collective-permute-start.1
  14.7 0.7 constant_dynamic-update-slice_fusion
  15.4 0.0 slice-start
  15.4 1.0 slice_reduce_fusion.3
  16.4 0.0 copy-start.6
  16.4 0.0 slice-start.1
  16.4 3.7 constant_dynamic-update-slice_fusion.2
  20.2 0.0 collective-permute-done
  20.2 0.0 copy-done.6
  20.2 0.1 slice_compare_fusion.2
  20.3 0.0 collective-permute-done.1
  20.3 0.0 slice-done
  20.3 0.3 slice-done.1
  20.6 14.9 %fusion.50 = bf16[2048,1664]{1,0:T(8,128)(2,1)} fusion(bf16[2048,1664]{1,0:T(8,128)(2,1)S(1)} %bitcast.47, bf16[2051,1664]{1,0:T(8,128)(2,1)S(1)} %constant_dynamic-update-slice_fusion.1, f32[1664]{0:T(1024)S(1)} %get-tuple-element.7, f32[1664]{0:T(1024)S(1)} %get-tuple-element.8, f32[1664]{0:T(1024)S(1)} %get-tuple-element.6, ...), kind=kLoop, calls=%fused_computation.5.clone.clone.1 | loop fusion | flops 54525952 | bytes 34113152 | tf_op jit(solution)/shard_map/dot_general | solution.py:19
  35.5 140.4 %all-gather.2.cloned.1.call-done = bf16[2048,3072]{1,0:T(8,128)(2,1)} async-done(((bf16[2048,384]{1,0:T(8,128)(2,1)}), bf16[2048,3072]{1,0:T(8,128)(2,1)}) %all-gather.2.cloned.1.call-update) | async-done | bytes 12582928 | tf_op jit(solution)/shard_map/all_gather | solution.py:65
  175.9 28.5 %convolution_bitcast_fusion = f32[3072,1664]{0,1:T(8,128)} fusion(bf16[2048,3072]{1,0:T(8,128)(2,1)} %all-gather.2.cloned.1.call-done, bf16[2048,1664]{1,0:T(8,128)(2,1)} %fusion.50), kind=kOutput, calls=%fused_computation.6 | convolution fusion | flops 20937965568 | bytes 39845888 | tf_op jit(solution)/shard_map/dot_general | solution.py:19
  204.4 21.2 %copy.42 = f32[3072,1664]{1,0:T(8,128)} copy(f32[3072,1664]{0,1:T(8,128)} %convolution_bitcast_fusion) | data formatting | bytes 40894464
  225.6 0.0 copy-start.3
  225.6 0.0 reduce-scatter.4.cloned.1.call-update
  225.6 0.0 all-reduce.3.cloned.1.call-start
  225.7 1.7 copy-done.3
  227.4 3.0 copy.44
  230.3 110.6 %reduce-scatter.4.cloned.1.call-done = f32[192,1664]{1,0:T(8,128)} async-done(((f32[3072,1664]{1,0:T(8,128)}), f32[192,1664]{1,0:T(8,128)}) %reduce-scatter.4.cloned.1.call-update) | async-done | bytes 1277968
  340.9 0.0 copy-start.2
  340.9 3.7 fusion.30
  344.6 0.0 all-reduce.3.cloned.1.call-update
  344.7 0.2 all-reduce.5.cloned.1.call-start
  344.9 0.0 copy-done.2
  344.9 0.5 copy.43
  345.4 0.0 copy-done
  345.4 0.0 copy-start.1
  345.4 1.8 fusion.32
  347.3 0.1 copy-done.1
  347.4 2.9 fusion.23
  350.3 4.0 multiply_convert_fusion
  354.3 3.6 copy.29
  357.8 1.0 copy.33
  358.8 1.2 reshape.64
  360.1 0.0 copy-start.4
  360.1 0.0 all-reduce.5.cloned.1.call-update
  360.1 1.3 copy-done.4
  361.4 3.5 divide_bitcast_fusion
  364.9 3.1 dot_general.45
  368.1 2.1 fusion.21
  370.2 5.2 fusion.26
  375.4 1.0 copy.36
  376.4 0.0 copy-start.7
  376.4 0.0 copy-start.5
  376.5 2.3 reshape.65
  378.7 41.8 %all-reduce.3.cloned.1.call-done = bf16[192,192]{0,1:T(8,128)(2,1)} async-done(((bf16[192,192]{0,1:T(8,128)(2,1)}), bf16[192,192]{0,1:T(8,128)(2,1)}) %all-reduce.3.cloned.1.call-update) | async-done | bytes 73744 | tf_op jit(solution)/shard_map/psum | solution.py:83
  420.5 0.0 copy-done.7
  420.5 1.3 multiply_add_fusion.2
  421.9 124.9 %all-reduce.5.cloned.1.call-done = bf16[1664,416]{0,1:T(8,128)(2,1)} async-done(((bf16[1664,416]{0,1:T(8,128)(2,1)}), bf16[1664,416]{0,1:T(8,128)(2,1)}) %all-reduce.5.cloned.1.call-update) | async-done | bytes 1384464 | tf_op jit(solution)/shard_map/psum | solution.py:84
  546.8 0.0 copy-done.5
  546.8 1.6 multiply_add_fusion.1
  (4 shorter events, 0.0 us)
Async XLA Ops:
  7.2 338.3 %copy-start = (f32[192,192]{1,0:T(8,128)S(1)}, f32[192,192]{1,0:T(8,128)}, u32[]{:S(2)}) copy-start(f32[192,192]{1,0:T(8,128)} %param.14) | copy-start | bytes 442372
  7.2 168.7 %all-gather.2.cloned.1.call-start = ((), (), s32[]{:S(2)}) async-start(), calls=%async_computation.1 | async-start | bytes 14155776 | tf_op jit(solution)/shard_map/all_gather | solution.py:65
  7.9 333.0 %reduce-scatter.4.cloned.1.call-start = ((), (), s32[]{:S(2)}) async-start(), calls=%async_computation.4 | async-start | bytes 21725184
  8.7 11.5 %collective-permute-start = (s32[3]{0:T(128)S(1)}, s32[3]{0:T(128)S(1)}, u32[]{:S(2)}, u32[]{:S(2)}) collective-permute-start(s32[3]{0:T(128)S(1)} %slice.37), channel_id=1, source_target_pairs={{1,0},{2,1},{3,2},{4,3},{5,4},{6,5},{7,6},{8,7},{9,8},{10,9},{11,1... | collective-permute-start | bytes 44 | tf_op jit(solution)/shard_map/ppermute | solution.py:15
  12.7 7.5 %collective-permute-start.1 = (bf16[3,1664]{1,0:T(4,128)(2,1)S(1)}, bf16[3,1664]{1,0:T(4,128)(2,1)S(1)}, u32[]{:S(2)}, u32[]{:S(2)}) collective-permute-start(bf16[3,1664]{1,0:T(4,128)(2,1)S(1)} %slice.40), channel_id=1, source_target_pairs={{1,0},{2,1},{3,2},{4,3},{5,4},{6,5},{7,6},{8,7},{9,8},{10,9},{11,1... | collective-permute-start | bytes 29960 | tf_op jit(solution)/shard_map/ppermute | solution.py:15
  15.4 4.9 slice-start
  16.4 3.8 copy-start.6
  16.4 4.2 slice-start.1
  225.6 1.8 copy-start.3
  225.6 194.9 %all-reduce.3.cloned.1.call-start = ((), (), s32[]{:S(2)}) async-start(), calls=%async_computation.2 | async-start | bytes 196608 | tf_op jit(solution)/shard_map/psum | solution.py:83
  340.9 4.0 copy-start.2
  344.7 202.1 %all-reduce.5.cloned.1.call-start = ((), (), s32[]{:S(2)}) async-start(), calls=%async_computation.3 | async-start | bytes 2768896 | tf_op jit(solution)/shard_map/psum | solution.py:84
  345.4 2.0 copy-start.1
  360.1 1.3 copy-start.4
  376.4 44.1 %copy-start.7 = (f32[192,24]{0,1:T(8,128)S(1)}, f32[192,24]{0,1:T(8,128)}, u32[]{:S(2)}) copy-start(f32[192,24]{0,1:T(8,128)} %param.16) | copy-start | bytes 55300
  376.4 170.4 %copy-start.5 = (f32[1664,26]{0,1:T(8,128)S(1)}, f32[1664,26]{0,1:T(8,128)}, u32[]{:S(2)}) copy-start(f32[1664,26]{0,1:T(8,128)} %param.17) | copy-start | bytes 519172
Sparse Core Ops, SparseCore 0:
  10.2 165.6 all-gather.1
  225.7 115.1 reduce-scatter.3
  344.8 75.6 all-reduce.2
  423.1 123.6 all-reduce.4
where the time goes:
time: 556 us; the launch traced here: 555 us
  waiting for transfers between devices  418 us (75%)
  matrix products  48.2 us (9%)
  local copies, waits for them, and re-layouts  47.3 us (9%)
  other arithmetic  21.4 us (4%)
  between operations  14 us (3%)
  starting transfers between devices  5.57 us (1%)
    all_gather x1, waiting for transfers between devices, shards(): lax.all_gather(layer_input, 'row', axis=1, tiled=True)  140 us
    psum x1, waiting for transfers between devices, shards(): lax.psum(right_factor_term.astype(jnp.bfloat16), 'col').astype(jnp.float32)  125 us
    unnamed x5, waiting for transfers between devices  111 us
    psum x1, waiting for transfers between devices, shards(): lax.psum(left_term.astype(jnp.bfloat16), 'row').astype(jnp.float32)  41.8 us
    unnamed x24, local copies, waits for them, and re-layouts  29.6 us
    dot_general x1, matrix products, contract_rows(): lax.dot_general(left, right, (((0,), (0,)), ((), ())), preferred_element_...  28.5 us
    dot_general x1, other arithmetic, contract_rows(): lax.dot_general(left, right, (((0,), (0,)), ((), ())), preferred_element_...  14.9 us
  transfers between devices with their start and end apart: 6, of which 4 were waited for; matrix products, arithmetic and copies ran while one was open for 11% of the time, Pallas kernels for 0%

commit v1 on v0

v1 whole, which is shorter than its diff:
```python
import jax
import jax.numpy as jnp
from jax import lax
from jax.experimental import pallas as pl
from jax.experimental.pallas import tpu as pltpu
from jax.sharding import PartitionSpec as P

MODEL_WIDTH = 3072
OUTPUT_CHANNELS = 13312
ZW = 6144
XW = 6656
TOK = 2048
FEAT = 384
CH = 1664
BL = 192
RB = 416
STRIPS = 4
RSHARE = 26
LSHARE = 24
HALO = 16
F32 = jnp.float32
BF16 = jnp.bfloat16
MESH = pl.DeviceIdType.MESH

N = 16
NCH = BL // N
GRAMS = (NCH, NCH + 1)
NALL = NCH + 2
SLOTS = 4
XFIRST = (False, False, True, True, True, False, False, True, False, False, False, False)
ORDER = (
    ("xo", 0), ("xo", 1), ("y", 0), ("y", 1), ("y", 2), ("conv", 0), ("xo", 2), ("y", 3),
    ("conv", 1), ("fo", 0), ("xq", 0), ("y", 4), ("conv", 2), ("fo", 1), ("y", 5), ("xq", 1),
    ("conv", 3), ("fo", 2), ("ys", 2), ("xo", 3), ("fq", 0), ("y", 6), ("xo", 4), ("fq", 1),
    ("y", 8), ("xq", 5), ("yf", 2), ("fo", 3), ("mul", 0), ("xo", 5), ("ys", 3), ("fo", 4),
    ("ex", 0), ("mul", 1), ("xq", 6), ("ex", 1), ("sz", 0), ("fq", 5), ("ys", 4), ("mul", 2),
    ("fo", 5), ("ex", 2), ("sz", 1), ("xq", 8), ("yf", 3), ("sy", 0), ("sz", 2), ("xo", 6),
    ("fq", 6), ("yf", 4), ("mul", 5), ("xo", 7), ("y", 7), ("ex", 5), ("sy", 1), ("fq", 8),
    ("mul", 3), ("fo", 6), ("xo", 8), ("y", 9), ("ex", 3), ("sz", 5), ("y", 10), ("sy", 2),
    ("fin", 0), ("mul", 4), ("fo", 7), ("xo", 9), ("ex", 4), ("sz", 3), ("ys", 7), ("fin", 1),
    ("mul", 6), ("xq", 9), ("ex", 6), ("sz", 4), ("fo", 8), ("sy", 5), ("xo", 10), ("sz", 6),
    ("yf", 7), ("sy", 3), ("fo", 9), ("fin", 2), ("xq", 10), ("fq", 9), ("y", 11), ("sy", 4),
    ("mul", 8), ("xo", 11), ("ex", 8), ("fin", 5), ("fo", 10), ("sy", 6), ("mul", 7),
    ("fq", 10), ("ex", 7), ("sz", 8), ("fin", 3), ("mul", 9), ("xq", 11), ("ex", 9), ("sz", 7),
    ("fo", 11), ("fin", 4), ("fin", 6), ("mul", 10), ("ex", 10), ("sz", 9), ("fq", 11),
    ("sy", 8), ("mulp", "near"), ("exp", "near"), ("sz", 10), ("mulp", "far"), ("exp", "far"),
    ("sy", 7), ("scp", "near"), ("sy", 9), ("fin", 8), ("scp", "far"), ("fin", 7), ("sy", 10),
    ("fin", 9), ("fin", 10),
)
POOL = 40
NGROUP = 100
LAST = NCH - 1


def contract(a, b, da, db):
    return lax.dot_general(a, b, (((da,), (db,)), ((), ())), preferred_element_type=F32)


def split(v):
    high = v.astype(BF16)
    return high, (v - high.astype(F32)).astype(BF16)


def contract3(a, b, da, db):
    small = contract(a[0], b[1], da, db) + contract(a[1], b[0], da, db)
    return contract(a[0], b[0], da, db) + small


class Messages:
    def __init__(self, send_sems, recv_sems):
        self.send_sems, self.recv_sems = send_sems, recv_sems
        self.copies = []
        self.groups = {}
        self.sent = set()
        self.arrived = set()

    def make(self, key, src, dst, device):
        i = len(self.copies)
        if i >= POOL:
            self.release(i - POOL)
        group = self.groups.setdefault(key, len(self.groups))
        assert group < NGROUP
        copy = pltpu.make_async_remote_copy(
            src_ref=src,
            dst_ref=dst,
            send_sem=self.send_sems.at[i % POOL],
            recv_sem=self.recv_sems.at[group],
            device_id=device,
            device_id_type=MESH,
        )
        copy.start()
        self.copies.append(copy)
        return i

    def release(self, i):
        if i not in self.sent:
            self.sent.add(i)
            self.copies[i].wait_send()

    def arrive(self, key, like, device):
        if key not in self.arrived:
            self.arrived.add(key)
            pltpu.make_async_remote_copy(
                src_ref=like,
                dst_ref=like,
                send_sem=self.send_sems.at[0],
                recv_sem=self.recv_sems.at[self.groups[key]],
                device_id=device,
                device_id_type=MESH,
            ).wait_recv()


def step_kernel(
    x_hbm, cg_hbm, taps_hbm, ids_hbm, right_basis_hbm, first_hbm, second_hbm, right_stat_hbm,
    left_basis_hbm, left_stat_hbm,
    first_out, second_out, direction_out, new_left_out, new_right_out,
    *scratch,
):
    (x_v, cg, taps_ref, ids_ref, proj, ids_col, ids_after, xt, stage, xrecv, zsend, zrecv, zown,
     ysend, yrecv, qsend, qrecv, qown, gsend, grecv, dsend, drecv, grad_ref, first, second, work,
     right_basis, right_stat, left_basis, left_stat, left_send, left_recv,
     local_sems, send_sems, recv_sems, dsend_sems, drecv_sems) = scratch

    row = lax.axis_index("row")
    col = lax.axis_index("col")
    y_hi, x = row // 4, row % 4
    y_lo, z, core = col // 8, (col // 2) % 4, col % 2
    r_left = y_hi * 4 + (x + 3) % 4
    r_right = y_hi * 4 + (x + 1) % 4
    r_far = y_hi * 4 + (x + 2) % 4

    def across(r):
        return (r + 4) % 8

    d_row = [((row + k) % 8, col) for k in range(1, 8)]
    d_y = (across(row), col)
    d_right = (r_right, col)
    d_left = (r_left, col)
    d_sib = (row, y_lo * 8 + z * 2 + (1 - core))
    d_z = [(row, y_lo * 8 + ((z + k) % 4) * 2 + core) for k in (1, 2, 3)]
    d_ylo = (row, (1 - y_lo) * 8 + z * 2 + core)
    d_prev = (row, (col + 15) % 16)
    d_next = (row, (col + 1) % 16)

    barrier = pltpu.get_barrier_semaphore()
    peers = [*d_row, d_sib, *d_z, d_ylo, d_prev, d_next]
    for d in peers:
        pl.semaphore_signal(barrier, inc=1, device_id=d, device_id_type=MESH)

    loads = [
        pltpu.make_async_copy(src, dst, local_sems.at[i])
        for i, (src, dst) in enumerate(
            [
                (x_hbm, x_v),
                (cg_hbm, cg.at[pl.ds(0, TOK)]),
                (taps_hbm, taps_ref),
                (ids_hbm, ids_ref),
                (right_basis_hbm, right_basis),
                (first_hbm, first),
                (second_hbm, second),
                (right_stat_hbm, right_stat),
                (left_basis_hbm, left_basis),
                (left_stat_hbm, left_stat),
            ]
        )
    ]
    load_x, early_loads, later_loads = loads[0], loads[1:4], loads[4:]
    load_x.start()
    for c in early_loads:
        c.start()
    load_x.wait()
    for b in range(3):
        turned = jnp.transpose(x_v[:, 128 * b : 128 * (b + 1)])
        for g in range(8):
            at = 8 * b + g
            xt[at % NCH, row, N * (at // NCH) : N * (at // NCH + 1), :] = turned[
                N * g : N * (g + 1), :
            ]
    pl.semaphore_wait(barrier, len(peers))

    msgs = Messages(send_sems, recv_sems)
    done = {}

    rel = [row, r_left, r_right, across(row), across(r_left), across(r_right), r_far, across(r_far)]

    def send(kind, j, r, device):
        msgs.make((kind, j), xt.at[j, r], xt.at[j, r], device)

    def sent_round(kind, j):
        msgs.arrive((kind, j), xt.at[j, pl.ds(0, 2)], d_right)

    def forward(kind, out, j, left, right):
        sent_round(kind, j)
        half_a, half_b = xt.at[j, left, pl.ds(0, N)], xt.at[j, right, pl.ds(N, N)]
        msgs.make((out, j), half_a, half_a, d_right)
        msgs.make((out, j), half_b, half_b, d_left)

    def send_own(j):
        send("xo", j, row, d_right)
        send("xo", j, row, d_left)

    def forward_own(j):
        forward("xo", "fo" if XFIRST[j] else "far", j, r_left, r_right)

    def send_y(j):
        send("y", j, row, d_y)

    def send_across(j):
        msgs.arrive(("y", j), xt.at[j, 0], d_y)
        send("xq", j, across(row), d_right)
        send("xq", j, across(row), d_left)

    def forward_across(j):
        forward("xq", "far", j, across(r_left), across(r_right))

    def send_y_sides(j):
        sent_round("xo", j)
        send("y", j, r_left, d_y)
        send("y", j, r_right, d_y)

    def send_y_far(j):
        msgs.arrive(("fo", j), xt.at[j, 0], d_right)
        send("y", j, r_far, d_y)

    def gathered(j):
        if XFIRST[j]:
            msgs.arrive(("y", j), xt.at[j, pl.ds(0, 4)], d_y)
        else:
            msgs.arrive(("far", j), xt.at[j, pl.ds(0, 2)], d_right)

    products = []
    exchanged = {}
    added = set()

    def place_in_stage(j):
        m = len(products)
        if m >= SLOTS:
            assert products[m - SLOTS] in added
            for i in exchanged[products[m - SLOTS]]:
                msgs.release(i)
        products.append(j)
        return m % SLOTS

    def over_tiles(tile):
        def step(i, _):
            tile(pl.ds(pl.multiple_of(i * 512, 512), 512), 512)
            return 0

        lax.fori_loop(0, CH // 512, step, 0)
        tile(pl.ds(CH // 512 * 512, CH % 512), CH % 512)

    def multiply(j):
        gathered(j)
        s = place_in_stage(j)

        def tile(cols, width):
            out = jnp.dot(
                xt[j].reshape(16 * N, TOK), proj[:, cols], preferred_element_type=F32
            ).reshape(8, 2, N, width)
            stage[s, 0, :, :, cols] = out[:, 0]
            stage[s, 1, :, :, cols] = out[:, 1]

        over_tiles(tile)

    def may_exchange(j):
        m = products.index(j)
        assert m < 2 or products[m - 2] in added
        return m % SLOTS

    def exchange(j):
        s = may_exchange(j)
        exchanged[j] = [msgs.make(("ex", j), stage.at[s, 1 - core], xrecv.at[s], d_sib)]

    def take_exchange(j):
        msgs.arrive(("ex", j), xrecv.at[0], d_sib)
        added.add(j)

    def both_cores(j, at):
        s = products.index(j) % SLOTS
        if j in GRAMS:
            return stage[s, 0, at] + grecv[j - NCH, at].astype(F32)
        return stage[s, core, at] + xrecv[s, at]

    def scatter_z(j):
        if j < NCH:
            take_exchange(j)
        for k in (2, 1, 3):
            for yl in range(2):
                zsend[j, k - 1, yl] = both_cores(j, yl * 4 + (z + k) % 4).astype(BF16)
            msgs.make(("z", j), zsend.at[j, k - 1], zrecv.at[j, k - 1], d_z[k - 1])
        for yl in range(2):
            zown[j, yl] = both_cores(j, yl * 4 + z)

    def rows(j):
        if j < NCH:
            return grad_ref.at[N * j : N * (j + 1)]
        return work.at[N * (j - NCH) : N * (j - NCH + 1)]

    def scatter_y(j):
        msgs.arrive(("z", j), zrecv.at[j], d_z[0])

        def total(yl):
            parts = [zrecv[j, k, yl].astype(F32) for k in range(3)]
            return (parts[0] + parts[1]) + (parts[2] + zown[j, yl])

        ysend[j] = total(1 - y_lo).astype(BF16)
        msgs.make(("ys", j), ysend.at[j], yrecv.at[j], d_ylo)
        rows(j)[...] = total(y_lo)

    def finish(j):
        msgs.arrive(("ys", j), yrecv.at[j], d_ylo)
        rows(j)[...] = rows(j)[...] + yrecv[j].astype(F32)

    def scatter_y_first(j):
        for k in range(4):
            qsend[k] = both_cores(j, (1 - y_lo) * 4 + k).astype(BF16)
        msgs.make(("qy", j), qsend, qrecv, d_ylo)
        for k in range(4):
            qown[k] = both_cores(j, y_lo * 4 + k)

    def scatter_z_last(j):
        msgs.arrive(("qy", j), qrecv, d_ylo)
        for k in (2, 1, 3):
            at = (z + k) % 4
            zsend[j, k - 1, 0] = (qown[at] + qrecv[at].astype(F32)).astype(BF16)
            msgs.make(("z", j), zsend.at[j, k - 1, 0], zrecv.at[j, k - 1, 0], d_z[k - 1])
        rows(j)[...] = qown[z] + qrecv[z].astype(F32)

    def finish_z(j):
        msgs.arrive(("z", j), zrecv.at[j, :, 0], d_z[0])
        parts = [zrecv[j, k, 0].astype(F32) for k in range(3)]
        rows(j)[...] = (rows(j)[...] + parts[0]) + (parts[1] + parts[2])

    PARTS = {"near": (0, 6), "far": (6, 2)}
    mine = col // 2

    def multiply_part(part):
        first_rel, count = PARTS[part]
        if part == "near":
            s = place_in_stage(LAST)
        else:
            gathered(LAST)
            s = products.index(LAST) % SLOTS
        lhs = jnp.concatenate([xt[LAST, r] for r in rel[first_rel : first_rel + count]], 0)

        def tile(cols, width):
            out = jnp.dot(lhs, proj[:, cols], preferred_element_type=F32)
            out = out.reshape(count, 2, N, width)
            stage[s, 0, first_rel : first_rel + count, :, cols] = out[:, 0]
            stage[s, 1, first_rel : first_rel + count, :, cols] = out[:, 1]

        over_tiles(tile)

    def exchange_part(part):
        s = may_exchange(LAST)
        at = pl.ds(*PARTS[part])
        i = msgs.make((part, "ex"), stage.at[s, 1 - core, at], xrecv.at[s, at], d_sib)
        exchanged.setdefault(LAST, []).append(i)

    def direct(k):
        r = rel[k]
        return pltpu.make_async_remote_copy(
            src_ref=dsend.at[k],
            dst_ref=drecv.at[mine],
            send_sem=dsend_sems.at[k],
            recv_sem=drecv_sems.at[mine],
            device_id=(row, (r // 4) * 8 + (r % 4) * 2 + core),
            device_id_type=MESH,
        )

    def scatter_part(part):
        first_rel, count = PARTS[part]
        msgs.arrive((part, "ex"), xrecv.at[0, pl.ds(0, count)], d_sib)
        if (part, "ex") in msgs.arrived and len(exchanged[LAST]) == 2:
            added.add(LAST)
        for k in range(first_rel, first_rel + count):
            total = both_cores(LAST, k)
            dsend[k] = total.astype(BF16)

            @pl.when(rel[k] == mine)
            def _():
                rows(LAST)[...] = total

            @pl.when(rel[k] != mine)
            def _():
                direct(k).start()

    def finish_last():
        for k in range(1, 8):
            sender = (mine + k) % 8
            pltpu.make_async_remote_copy(
                src_ref=dsend.at[0],
                dst_ref=drecv.at[sender],
                send_sem=dsend_sems.at[0],
                recv_sem=drecv_sems.at[sender],
                device_id=d_ylo,
                device_id_type=MESH,
            ).wait_recv()
        parts = [drecv[(mine + k) % 8].astype(F32) for k in range(1, 8)]
        total = (parts[0] + parts[1]) + (parts[2] + parts[3]) + (parts[4] + parts[5])
        rows(LAST)[...] = rows(LAST)[...] + (total + parts[6])

    channel = row * CH + lax.broadcasted_iota(jnp.int32, (1, CH), 1)
    convolved = (channel >= ZW) & (channel < ZW + XW)

    def tap(k):
        return jnp.where(convolved, taps_ref[k : k + 1, :], F32(1.0 if k == 0 else 0.0))

    def number_columns():
        for q in range(TOK // 128):
            line = jnp.broadcast_to(ids_ref[q : q + 1, :].astype(F32), (128, 128))
            ids_col[128 * q : 128 * (q + 1), :] = jnp.transpose(line)

    def number_after():
        line = jnp.where(col == 15, F32(-1.0), ids_after[0:1, :].astype(F32))
        ids_col[TOK : TOK + HALO, :] = jnp.transpose(jnp.broadcast_to(line, (128, 128)))[:HALO]

    def convolve(part):
        count = 64
        if part == 0:
            for c in later_loads:
                c.start()
            for c in early_loads:
                c.wait()
            number_columns()
        taps = [tap(k) for k in range(4)]

        def step(i, _):
            t = pl.multiple_of(i * count, count)
            ids = ids_col[pl.ds(t, count + HALO), :]
            same = [ids[k : k + count] == ids[:count] for k in range(1, 4)]
            for b in range(CH // 128):
                lanes = slice(128 * b, 128 * (b + 1))
                g = cg[pl.ds(t, count + HALO), lanes].astype(F32)
                total = taps[0][:, lanes] * g[:count]
                for k in range(1, 4):
                    term = taps[k][:, lanes] * g[k : k + count]
                    total = total + jnp.where(same[k - 1], term, F32(0.0))
                proj[pl.ds(t, count), lanes] = total.astype(BF16)
            return 0

        if part == 3:
            msgs.arrive("halo", cg.at[pl.ds(TOK, HALO)], d_prev)
            msgs.arrive("ids", ids_after, d_prev)
            number_after()
        lax.fori_loop(8 * part, 8 * part + 8, step, 0)
        if part == 3:
            for c in later_loads:
                c.wait()
            for t in range(STRIPS):
                high, low = split(right_basis[:, strip(t)])
                cg[strip(t), :RB] = high
                cg[strip(t), 512 : 512 + RB] = low

    def strip(t):
        return slice(RB * t, RB * (t + 1))

    def q_right(t):
        return cg[strip(t), :RB], cg[strip(t), 512 : 512 + RB]

    msgs.make("halo", cg_hbm.at[pl.ds(0, HALO)], cg.at[pl.ds(TOK, HALO)], d_prev)
    msgs.make("ids", ids_hbm.at[pl.ds(0, 8)], ids_after, d_prev)
    steps = {
        "xo": send_own,
        "fo": forward_own,
        "y": send_y,
        "xq": send_across,
        "fq": forward_across,
        "ys": send_y_sides,
        "yf": send_y_far,
        "conv": convolve,
        "mul": multiply,
        "ex": exchange,
        "sz": scatter_z,
        "sy": scatter_y,
        "fin": finish,
        "mulp": multiply_part,
        "exp": exchange_part,
        "scp": scatter_part,
    }
    for name, j in ORDER:
        steps[name](j)
    finish_last()

    place = lax.broadcasted_iota(jnp.int32, (RB, 16 * 32), 1)
    source = lax.broadcasted_iota(jnp.int32, (RB, 16 * 32), 0)
    chosen = (place % 32 < RSHARE) & (place // 32 * RSHARE + place % 32 == source)
    one_hot = jnp.where(chosen, F32(1.0), F32(0.0)).astype(BF16)
    slots = [place_in_stage(j) for j in GRAMS]
    for t in range(STRIPS):
        band = grad_ref[:, strip(t)].astype(BF16)
        placed = jnp.dot(band, one_hot, preferred_element_type=F32).astype(BF16)
        block = contract(placed, band, 0, 0).reshape(8, 2, 2, N, RB)
        for h, s in enumerate(slots):
            even, odd = block[:, 0, h], block[:, 1, h]
            stage[s, 0, :, :, strip(t)] = jnp.where(core == 0, even, odd)
            gsend[h, :, :, strip(t)] = jnp.where(core == 0, odd, even).astype(BF16)
    for h in range(2):
        msgs.make(("gram", h), gsend.at[h], grecv.at[h], d_sib)

    rounded = grad_ref[...].astype(BF16)
    left = contract(rounded, rounded, 1, 1)
    for r in range(8):
        share = left[LSHARE * r : LSHARE * (r + 1)]
        left_send[r] = jnp.concatenate([share, jnp.zeros((32 - LSHARE, BL), F32)], 0).astype(BF16)
    for k in range(1, 8):
        msgs.make("left", left_send.at[(row + k) % 8], left_recv.at[k - 1], d_row[k - 1])

    q_left = split(left_basis[...])
    msgs.arrive(("gram", 0), grecv.at[0], d_sib)
    scatter_z(GRAMS[0])
    msgs.arrive(("gram", 1), grecv.at[1], d_sib)
    scatter_y_first(GRAMS[1])
    grad_parts = split(grad_ref[...])
    grad_ref[...] = contract3(q_left, grad_parts, 0, 0)

    def moments(t):
        rotated = contract3(split(grad_ref[:, strip(t)]), q_right(t), 1, 1)
        new_first = 0.9 * first[:, strip(t)] + 0.1 * rotated
        new_second = 0.95 * second[:, strip(t)] + 0.05 * rotated * rotated
        first[:, strip(t)] = new_first
        second[:, strip(t)] = new_second
        grad_ref[:, strip(t)] = new_first / (jnp.sqrt(new_second) + 1e-08)

    for t in range(STRIPS):
        moments(t)
    scatter_z_last(GRAMS[1])
    stores = [
        pltpu.make_async_copy(src, dst, local_sems.at[10 + i])
        for i, (src, dst) in enumerate(
            [
                (first, first_out),
                (second, second_out),
                (grad_ref, direction_out),
                (left_stat, new_left_out),
                (right_stat, new_right_out),
            ]
        )
    ]
    stores[0].start()
    stores[1].start()
    grad_ref[...] = contract3(q_left, split(grad_ref[...]), 1, 0)
    scatter_y(GRAMS[0])
    for t in range(STRIPS):
        grad_ref[:, strip(t)] = contract3(split(grad_ref[:, strip(t)]), q_right(t), 1, 0)
    stores[2].start()

    msgs.arrive("left", left_recv, d_row[0])
    total = left_send[row].astype(F32)
    for k in range(7):
        total = total + left_recv[k].astype(F32)
    left_stat[...] = 0.9 * left_stat[...] + 0.1 * (total[:LSHARE] / OUTPUT_CHANNELS)
    stores[3].start()

    finish_z(GRAMS[1])
    finish(GRAMS[0])
    right_stat[...] = 0.9 * right_stat[...] + 0.1 * (work[:RSHARE, :] / MODEL_WIDTH)
    stores[4].start()
    for i in range(len(msgs.copies)):
        msgs.release(i)
    for k in range(8):

        @pl.when(rel[k] != mine)
        def _():
            direct(k).wait_send()

    for c in stores:
        c.wait()


PIECES = 4


def copy_kernel(*refs):
    count = (len(refs) - 2) // 3
    in_sems, out_sems = refs[-2:]
    loads, stores = [], []
    for src, dst, held in zip(refs[:count], refs[count : 2 * count], refs[2 * count : -2]):
        pieces = PIECES if src.shape[0] == BL else 1
        height = src.shape[0] // pieces
        for i in range(pieces):
            at = pl.ds(i * height, height)
            k = len(loads)
            loads.append(pltpu.make_async_copy(src.at[at], held.at[at], in_sems.at[k]))
            stores.append(pltpu.make_async_copy(held.at[at], dst.at[at], out_sems.at[k]))
    for c in loads:
        c.start()
    for c, d in zip(loads, stores):
        c.wait()
        d.start()
    for d in stores:
        d.wait()


def shards(
    layer_input,
    conv_grad,
    conv_kernel,
    segment_ids,
    left_basis,
    right_basis,
    left_stat,
    right_stat,
    first_moment,
    second_moment,
):
    any_spec = pl.BlockSpec(memory_space=pl.ANY)
    block = jax.ShapeDtypeStruct((BL, CH), F32)
    out_shape = [
        block,
        block,
        block,
        jax.ShapeDtypeStruct((LSHARE, BL), F32),
        jax.ShapeDtypeStruct((RSHARE, CH), F32),
    ]
    results = pl.pallas_call(
        step_kernel,
        out_shape=out_shape,
        in_specs=[any_spec] * 10,
        out_specs=[any_spec] * 5,
        scratch_shapes=[
            pltpu.VMEM((TOK, FEAT), BF16),
            pltpu.VMEM((TOK + HALO, CH), BF16),
            pltpu.VMEM((4, CH), F32),
            pltpu.VMEM((TOK // 128, 128), jnp.int32),
            pltpu.VMEM((TOK, CH), BF16),
            pltpu.VMEM((TOK + HALO, 128), F32),
            pltpu.VMEM((8, 128), jnp.int32),
            pltpu.VMEM((NCH, 8, 2 * N, TOK), BF16),
            pltpu.VMEM((SLOTS, 2, 8, N, CH), F32),
            pltpu.VMEM((SLOTS, 8, N, CH), F32),
            pltpu.VMEM((NALL, 3, 2, N, CH), BF16),
            pltpu.VMEM((NALL, 3, 2, N, CH), BF16),
            pltpu.VMEM((NALL, 2, N, CH), F32),
            pltpu.VMEM((NALL, N, CH), BF16),
            pltpu.VMEM((NALL, N, CH), BF16),
            pltpu.VMEM((4, N, CH), BF16),
            pltpu.VMEM((4, N, CH), BF16),
            pltpu.VMEM((4, N, CH), F32),
            pltpu.VMEM((2, 8, N, CH), BF16),
            pltpu.VMEM((2, 8, N, CH), BF16),
            pltpu.VMEM((8, N, CH), BF16),
            pltpu.VMEM((8, N, CH), BF16),
            pltpu.VMEM((BL, CH), F32),
            pltpu.VMEM((BL, CH), F32),
            pltpu.VMEM((BL, CH), F32),
            pltpu.VMEM((2 * N, CH), F32),
            pltpu.VMEM((RB, CH), F32),
            pltpu.VMEM((RSHARE, CH), F32),
            pltpu.VMEM((BL, BL), F32),
            pltpu.VMEM((LSHARE, BL), F32),
            pltpu.VMEM((8, 32, BL), BF16),
            pltpu.VMEM((7, 32, BL), BF16),
            pltpu.SemaphoreType.DMA((15,)),
            pltpu.SemaphoreType.DMA((POOL,)),
            pltpu.SemaphoreType.DMA((NGROUP,)),
            pltpu.SemaphoreType.DMA((8,)),
            pltpu.SemaphoreType.DMA((8,)),
        ],
        name="step",
        cost_estimate=pl.CostEstimate(
            flops=2 * MODEL_WIDTH * TOK * CH, bytes_accessed=20_000_000, transcendentals=0
        ),
        compiler_params=pltpu.CompilerParams(
            collective_id=0, has_side_effects=True, vmem_limit_bytes=63 << 20
        ),
    )(
        layer_input,
        conv_grad,
        conv_kernel,
        segment_ids.reshape(TOK // 128, 128),
        right_basis.T,
        first_moment,
        second_moment,
        right_stat.T,
        left_basis,
        left_stat.T,
    )
    first, second, direction, new_left, new_right = pl.pallas_call(
        copy_kernel,
        out_shape=out_shape,
        in_specs=[any_spec] * 5,
        out_specs=[any_spec] * 5,
        scratch_shapes=[
            *[pltpu.VMEM(a.shape, F32) for a in out_shape],
            pltpu.SemaphoreType.DMA((3 * PIECES + 2,)),
            pltpu.SemaphoreType.DMA((3 * PIECES + 2,)),
        ],
        name="hand_over",
    )(*results)
    return new_left.T, new_right.T, first, second, direction


def solution(mesh):
    placed = (
        P("col", "row"),
        P("col", "row"),
        P(None, "row"),
        P("col"),
        P("col", None),
        P("row", None),
        P("col", "row"),
        P("row", "col"),
        P("col", "row"),
        P("col", "row"),
    )
    return jax.shard_map(
        shards,
        mesh=mesh,
        in_specs=placed,
        out_specs=(
            P("col", "row"),
            P("row", "col"),
            P("col", "row"),
            P("col", "row"),
            P("col", "row"),
        ),
        check_vma=False,
    )
```

time: 556 us -> 130 us (0.23)
  waiting for transfers between devices: 418 us -> 0 us
  Pallas kernels: 0 us -> 129 us
  matrix products: 48.2 us -> 0 us
  local copies, waits for them, and re-layouts: 47.3 us -> 0 us
  other arithmetic: 21.4 us -> 0 us
  between operations: 14 us -> 0.8 us
  starting transfers between devices: 5.57 us -> 0 us
    psum x2 -> x0, waiting for transfers between devices: 167 us -> none  [the longest x1 125 us: shards(): lax.psum(right_factor_term.astype(jnp.bfloat16), 'col').astype(jnp.float32)]
    all_gather x1 -> x0, waiting for transfers between devices: 140 us -> none  [shards(): lax.all_gather(layer_input, 'row', axis=1, tiled=True)]
    pallas_call x0 -> x2, Pallas kernels: none -> 129 us  [the longest x1 126 us: shards(): pl.pallas_call(step_kernel, out_shape=out_shape, in_specs=[any_spec] * 10...]
    unnamed x5 -> x0, waiting for transfers between devices: 111 us -> none
    dot_general x7 -> x0, matrix products: 48.2 us -> none  [the longest x1 28.5 us: contract_rows(): lax.dot_general(left, right, (((0,), (0,)), ((), ())), preferred_element_...]
    unnamed x24 -> x0, local copies, waits for them, and re-layouts: 29.6 us -> none
    dot_general x2 -> x0, other arithmetic: 18.4 us -> none  [the longest x1 14.9 us: contract_rows(): lax.dot_general(left, right, (((0,), (0,)), ((), ())), preferred_element_...]
    reshape x3 -> x0, local copies, waits for them, and re-layouts: 6.47 us -> none  [the longest x1 2.97 us: shards(): right_q = right_basis.reshape(nstrips, right_block_index, right_block_index)]
  transfers between devices with their start and end apart: 6 -> 0, of which waited for: 4 -> 0; matrix products, arithmetic and copies ran while one was open for 11% -> 0% of each run, Pallas kernels for 0% -> 0%
where the time goes in v1:
time: 130 us
  Pallas kernels  129 us (99%)
    pallas_call x1, Pallas kernels, shards(): pl.pallas_call(step_kernel, out_shape=out_shape, in_specs=[any_spec] * 10...  126 us
    pallas_call x1, Pallas kernels, shards(): pl.pallas_call(copy_kernel, out_shape=out_shape, in_specs=[any_spec] * 5,...  3.62 us

profile of v1, /device:TPU:1, one launch (start us, length us, event | category | flops | bytes accessed | tf_op | source)
XLA Modules:
  0.0 130.2 jit_solution(14467472348270217796)
XLA Ops:
  0.6 125.8 %step.1 = (f32[192,1664]{1,0:T(8,128)}, f32[192,1664]{1,0:T(8,128)}, f32[192,1664]{1,0:T(8,128)}, f32[24,192]{1,0:T(8,128)}, f32[26,1664]{1,0:T(8,128)}) custom-call(bf16[2048,384]{1,0:T(8,128)(2,1)} %x_hbm.1, bf16[2048,1664]{1,0:T(8,128)(2,1)} %cg_hbm.1, f32[4,1664]{1,0:T(4,128)} %taps_hbm.1, s32[16,128]{1,0:T(8,128)} %bitcast.11, f32[416,1664]{1,0:T(8,128)} %bitcast.6, ...), custom_call_target="tpu_custom_call" | custom-call | flops 20937965568 | bytes 20000000 | tf_op jit(solution)/shard_map/step/pallas_call | solution.py:616
  126.5 3.6 %hand_over.1 = (f32[192,1664]{1,0:T(8,128)}, f32[192,1664]{1,0:T(8,128)}, f32[192,1664]{1,0:T(8,128)}, f32[24,192]{1,0:T(8,128)}, f32[26,1664]{1,0:T(8,128)}) custom-call(f32[192,1664]{1,0:T(8,128)} %get-tuple-element.15.refs_0_, f32[192,1664]{1,0:T(8,128)} %get-tuple-element.16.refs_1_, f32[192,1664]{1,0:T(8,128)} %get-tuple-element.17.refs_2_, ...), custom_call_target="tpu_custom_call" | custom-call | tf_op jit(solution)/shard_map/hand_over/pallas_call | solution.py:679
